TPU v7x, 256 devices: a whole 4x4x8 slice. The times are simulated.
256 devices in a mesh: row: 16 (over z, y_lo), pair: 16 (over y_hi, x, core).
Axes of the slice: x: 4, y: 4 (y_hi: 2, y_lo: 2; y = y_hi * 2 + y_lo), z: 8, core: 2. Of those that a mesh axis runs over, the one named last changes fastest.
Arguments:
- slab: float32 [16384, 8192], P('row', 'pair'), may hold values from -400 to 400
- moves: int32 [1, 16], P(None, 'pair'), may hold values from 0 to 1, as said below
Outputs:
- rotated_slab: float32 [16384, 8192], P('row', 'pair')
Inputs may be any that keep to these rules, and one draw needn't show every extreme that they name: Every row of moves holds both values.
All inputs are finite; a program needn't handle non-finite values.
Results may differ from a plain program's by a relative error of at most 0.0003.
Values sent between devices are 32-bit elements; how exact they have to be, the bound alone decides.
A program may use at most 64 MiB of HBM per device.

v0:
```python
import jax
import jax.numpy as jnp
from jax import lax
from jax.sharding import PartitionSpec as P

ITERS = 3
ROUNDS = 2


epsilon = 1e-06


def from_behind(block, axis, distance):
    devices = range(lax.axis_size(axis))
    route = [((i - distance) % len(devices), i) for i in devices]
    return lax.ppermute(block, axis, route)


def product(left_side, right_side):
    return jnp.dot(
        left_side, right_side, precision=lax.Precision.HIGHEST, preferred_element_type=jnp.float32
    )


def gram_partial(pair_block):
    return lax.dot_general(
        pair_block,
        pair_block,
        (((0,), (0,)), ((), ())),
        precision=lax.Precision.HIGHEST,
        preferred_element_type=jnp.float32,
    )


def inverse_full(gram_full):
    width = gram_full.shape[0]
    gram_scale = jnp.sqrt(jnp.sum(gram_full * gram_full) + epsilon)
    powers = gram_full / gram_scale
    identity = jnp.eye(width, dtype=jnp.float32)
    inverse = identity
    for iteration in range(ITERS):
        if iteration == 0:
            tangent = 0.5 * (3.0 * identity - powers)
            inverse = tangent
        else:
            tangent = 0.5 * (3.0 * identity - product(inverse, powers))
            inverse = product(tangent, inverse)
        if iteration + 1 < ITERS:
            powers = product(tangent, powers)
    return (inverse, gram_scale)


def local(slab, moves):
    rows_here, width = slab.shape
    half_width = width // 2
    total_rows = rows_here * lax.axis_size("row")
    pair_block = slab
    for round_index in range(ROUNDS):
        partial_value = gram_partial(pair_block)
        gram_whole = lax.psum(partial_value, "row")
        inverse, gram_scale = inverse_full(gram_whole)
        rotated = product(pair_block, inverse)
        rotated = rotated * jnp.sqrt(total_rows / gram_scale)
        if round_index + 1 < ROUNDS:
            move_flag = moves[round_index, 0]
            lead_block = rotated[:, :half_width]
            trail_block = rotated[:, half_width:]
            forward = jnp.where(move_flag == 0, lead_block, trail_block)
            backward = jnp.where(move_flag == 0, trail_block, lead_block)
            arrived_forward = from_behind(forward, "pair", 1)
            arrived_backward = from_behind(backward, "pair", -1)
            pair_block = jnp.concatenate([arrived_forward, arrived_backward], axis=1)
        else:
            pair_block = rotated
    return pair_block


def solution(mesh):
    placed = (P("row", "pair"), P(None, "pair"))
    return jax.shard_map(
        local, mesh=mesh, in_specs=placed, out_specs=P("row", "pair"), check_vma=False
    )
```

profile of v0, /device:TPU:8, one launch (start us, length us, event | category | flops | bytes accessed | tf_op | source)
XLA Modules:
  0.0 371.6 jit_solution(1708957785043683818)
XLA Ops:
  6.5 1.6 copy-done
  8.1 4.5 %fusion.52 = f32[512,512]{1,0:T(8,128)} fusion(f32[1024,512]{1,0:T(8,128)S(1)} %copy-done), kind=kOutput, calls=%fused_computation.63 | convolution fusion | flops 3221225472 | bytes 3145728 | tf_op jit(solution)/shard_map/dot_general | solution.py:26
  13.6 141.3 %all-reduce.3.cloned.1.call-done = f32[512,512]{1,0:T(8,128)} async-done(((f32[512,512]{1,0:T(8,128)}), f32[512,512]{1,0:T(8,128)}) %all-reduce.3.cloned.1.call-update) | async-done | bytes 1048592 | tf_op jit(solution)/shard_map/psum | solution.py:60
  155.0 2.1 multiply_reduce_fusion.1
  157.8 3.6 fusion.8
  161.4 2.0 fusion
  163.4 1.8 fusion.53
  165.2 1.9 fusion.5
  167.2 1.9 fusion.1
  169.0 1.8 fusion.54
  171.0 7.3 %multiply_bitcast_fusion = f32[1024,512]{0,1:T(8,128)S(1)} fusion(f32[512,512]{1,0:T(8,128)S(1)} %fusion.54, f32[1024,512]{1,0:T(8,128)S(1)} %copy-done, f32[]{:T(128)S(6)} %sqrt.13), kind=kOutput, calls=%fused_computation.6 | convolution fusion | flops 3221749760 | bytes 5242884 | tf_op jit(solution)/shard_map/dot_general | solution.py:20
  178.6 5.5 %collective-permute-start.1 = (f32[1024,256]{0,1:T(8,128)S(1)}, f32[1024,256]{0,1:T(8,128)S(1)}, u32[]{:S(2)}, u32[]{:S(2)}) collective-permute-start(f32[1024,256]{0,1:T(8,128)S(1)} %get-tuple-element.5), channel_id=1, source_target_pairs={{1,0},{2,1},{3,2},{4,3},{5,4},{6,5},{7,6},{8,7},{9,8},{10,9},{11,1... | collective-permute-start | bytes 3145736 | tf_op jit(solution)/shard_map/ppermute | solution.py:16
  184.1 12.3 %collective-permute-done = f32[1024,256]{0,1:T(8,128)S(1)} collective-permute-done((f32[1024,256]{0,1:T(8,128)S(1)}, f32[1024,256]{0,1:T(8,128)S(1)}, u32[]{:S(2)}, u32[]{:S(2)}) %collective-permute-start) | collective-permute-done | bytes 1048608 | tf_op jit(solution)/shard_map/ppermute | solution.py:16
  196.6 1.3 copy-done.1
  198.0 4.5 %fusion.55 = f32[512,512]{1,0:T(8,128)} fusion(f32[1024,512]{0,1:T(8,128)S(1)} %constant_dynamic-update-slice_fusion), kind=kOutput, calls=%fused_computation.66 | convolution fusion | flops 3221225472 | bytes 3145728 | tf_op jit(solution)/shard_map/dot_general | solution.py:26
  202.5 139.4 %all-reduce.5.cloned.1.call-done = f32[512,512]{1,0:T(8,128)} async-done(((f32[512,512]{1,0:T(8,128)}), f32[512,512]{1,0:T(8,128)}) %all-reduce.5.cloned.1.call-update) | async-done | bytes 1048592 | tf_op jit(solution)/shard_map/psum | solution.py:60
  341.9 2.1 multiply_reduce_fusion
  344.8 3.6 fusion.14
  348.4 2.0 fusion.2
  350.4 1.8 fusion.56
  352.2 1.9 fusion.11
  354.2 2.1 fusion.3
  356.3 1.8 fusion.57
  358.2 6.4 %convolution_multiply_fusion = f32[1024,512]{1,0:T(8,128)} fusion(f32[1024,512]{0,1:T(8,128)} %copy-done.1, f32[512,512]{1,0:T(8,128)S(1)} %fusion.57, f32[]{:T(128)S(6)} %sqrt.15), kind=kOutput, calls=%fused_computation.7 | convolution fusion | flops 3221749760 | bytes 5242884 | tf_op jit(solution)/shard_map/dot_general | solution.py:20
  (15 shorter events, 0.9 us)
Async XLA Ops:
  6.5 1.6 copy-start
  6.5 148.4 %all-reduce.3.cloned.1.call-start = ((), (), s32[]{:S(2)}) async-start(), calls=%async_computation | async-start | bytes 2097152 | tf_op jit(solution)/shard_map/psum | solution.py:60
  12.6 329.3 %all-reduce.5.cloned.1.call-start = ((), (), s32[]{:S(2)}) async-start(), calls=%async_computation.1 | async-start | bytes 2097152 | tf_op jit(solution)/shard_map/psum | solution.py:60
  157.8 3.6 copy-start.2
  178.5 17.9 %collective-permute-start = (f32[1024,256]{0,1:T(8,128)S(1)}, f32[1024,256]{0,1:T(8,128)S(1)}, u32[]{:S(2)}, u32[]{:S(2)}) collective-permute-start(f32[1024,256]{0,1:T(8,128)S(1)} %get-tuple-element.6), channel_id=1, source_target_pairs={{15,0},{0,1},{1,2},{2,3},{3,4},{4,5},{5,6},{6,7},{7,8},{8,9},{9,10... | collective-permute-start | bytes 3145736 | tf_op jit(solution)/shard_map/ppermute | solution.py:16
  178.6 17.9 %collective-permute-start.1 = (f32[1024,256]{0,1:T(8,128)S(1)}, f32[1024,256]{0,1:T(8,128)S(1)}, u32[]{:S(2)}, u32[]{:S(2)}) collective-permute-start(f32[1024,256]{0,1:T(8,128)S(1)} %get-tuple-element.5), channel_id=1, source_target_pairs={{1,0},{2,1},{3,2},{4,3},{5,4},{6,5},{7,6},{8,7},{9,8},{10,9},{11,1... | collective-permute-start | bytes 3145736 | tf_op jit(solution)/shard_map/ppermute | solution.py:16
  196.6 1.3 copy-start.1
  344.8 3.7 copy-start.3
Sparse Core Ops, SparseCore 0:
  12.8 142.1 all-reduce.2
  202.6 139.2 all-reduce.4
where the time goes:
time: 375 us; the launch traced here: 372 us
  waiting for transfers between devices  293 us (78%)
  matrix products  49 us (13%)
  between operations  16 us (4%)
  starting transfers between devices  5.91 us (2%)
  other arithmetic  4.49 us (1%)
    psum x2, waiting for transfers between devices, local(): gram_whole = lax.psum(partial_value, 'row')  281 us
    dot_general x14, matrix products, product(): jnp.dot(left_side, right_side, precision=lax.Precision.HIGHEST, preferred...  40 us
    ppermute x2, waiting for transfers between devices, from_behind(): return lax.ppermute(block, axis, route)  12.3 us
    dot_general x2, matrix products, gram_partial(): lax.dot_general(pair_block, pair_block, (((0,), (0,)), ((), ())), precisi...  9 us
  transfers between devices with their start and end apart: 4, of which 3 were waited for; matrix products, arithmetic and copies ran while one was open for 0% of the time, Pallas kernels for 0%

commit v1 on v0

v1 whole, which is shorter than its diff:
```python
import functools

import jax
import jax.numpy as jnp
from jax import lax
from jax.experimental import pallas as pl
from jax.experimental.pallas import tpu as pltpu
from jax.sharding import PartitionSpec as P

MESH = pl.DeviceIdType.MESH
F32 = jnp.float32
BF16 = jnp.bfloat16
N = 16
H = 256
W = 512
R = 1024
ROWS = 16384
EPS = 1e-06
T = 256
CHUNKS1 = (4, 3, 3)
CHUNKS2 = (2, 2)


def dot(a, b):
    return jnp.dot(a, b, preferred_element_type=F32)


def split(v):
    hi = v.astype(BF16)
    return hi, (v - hi.astype(F32)).astype(BF16)


def keep(ref, rows, v):
    hi, lo = split(v)
    ref[0, rows, :] = hi
    ref[1, rows, :] = lo


def product(a, rows, b, cols=slice(None)):
    ah, al = a[0, rows, :], a[1, rows, :]
    bh, bl = b[0, :, cols], b[1, :, cols]
    return dot(ah, bh) + (dot(ah, bl) + dot(al, bh))


def tiles(n):
    return [pl.ds(i * T, T) for i in range(n // T)]


def eye_tile(i):
    r = lax.broadcasted_iota(jnp.int32, (T, W), 0) + i * T
    c = lax.broadcasted_iota(jnp.int32, (T, W), 1)
    return jnp.where(r == c, 1.0, 0.0).astype(F32)


def newton_schulz(a, ah, a2, u, v, z2, z2h, yh, z):
    for rows in tiles(W):
        keep(ah, rows, a[rows, :])
    for rows in tiles(W):
        at = a[rows, :]
        sq = product(ah, rows, ah)
        a2[rows, :] = sq
        keep(u, rows, sq - 5.0 * at)
        keep(v, rows, sq - 4.0 * at)
    for i, rows in enumerate(tiles(W)):
        p = product(u, rows, v)
        t = (p + 7.0 * a2[rows, :] - 39.0 * a[rows, :] + 36.0 * eye_tile(i)) * 0.0625
        z2[rows, :] = t
        keep(z2h, rows, t)
    for rows in tiles(W):
        keep(yh, rows, product(z2h, rows, ah))
        keep(u, rows, product(z2h, rows, z2h))
    for rows in tiles(W):
        z[rows, :] = 1.5 * z2[rows, :] - 0.5 * product(u, rows, yh)


class Reduce:
    def __init__(self, r, nb, part, parts, whole, ss, rs, sa, ra):
        self.r, self.nb = r, nb
        self.part, self.parts, self.whole = part, parts, whole
        self.ss, self.rs, self.sa, self.ra = ss, rs, sa, ra

    def put(self, j, block):
        self.part[:, j] = block.reshape(N, 8, 128)

    def scatter(self):
        for d in ORDER:
            to = lax.rem(self.r + d, N)
            pltpu.make_async_remote_copy(
                src_ref=self.part.at[to],
                dst_ref=self.parts.at[N - d],
                send_sem=self.ss,
                recv_sem=self.rs,
                device_id={"row": to},
                device_id_type=MESH,
            ).start()

    def _all(self, src, dst, ss, rs):
        return pltpu.make_async_remote_copy(
            src_ref=src.at[pl.ds(1, N - 1)],
            dst_ref=dst.at[pl.ds(1, N - 1)],
            send_sem=ss,
            recv_sem=rs,
            device_id={"row": lax.rem(self.r + 1, N)},
            device_id_type=MESH,
        )

    def gather(self):
        self._all(self.part, self.parts, self.ss, self.rs).wait_recv()
        total = self.part[self.r]
        for d in range(1, N):
            total = total + self.parts[d]
        self.whole[self.r] = total
        for d in ORDER:
            to = lax.rem(self.r + d, N)
            pltpu.make_async_remote_copy(
                src_ref=self.whole.at[self.r],
                dst_ref=self.whole.at[self.r],
                send_sem=self.sa,
                recv_sem=self.ra,
                device_id={"row": to},
                device_id_type=MESH,
            ).start()

    def arrive(self):
        self._all(self.whole, self.whole, self.sa, self.ra).wait_recv()

    def get(self, j):
        return self.whole[:, j].reshape(128, 128)

    def drain(self):
        self._all(self.part, self.parts, self.ss, self.rs).wait_send()
        self._all(self.whole, self.whole, self.sa, self.ra).wait_send()


ORDER = (8, 7, 9, 6, 10, 5, 11, 4, 12, 3, 13, 2, 14, 1, 15)


def kernel(x_hbm, mv_ref, out_hbm, *refs):
    n_ar = len(CHUNKS1) + len(CHUNKS2)
    ar_bufs, refs = refs[: 3 * n_ar], refs[3 * n_ar :]
    (x, xh, xt, a, ah, a2, u, v, z2, z2h, yh, z, d_out, d_in,
     s_out, s_in, q_out, q_in, nh, qt, out,
     load_sem, out_sem, ss, rs, sa, ra, xs, xr) = refs
    r, p = lax.axis_index("row"), lax.axis_index("pair")
    odd = lax.rem(p, 2)
    slow = lax.rem(p + (N - 1) + 2 * odd, N)
    quick = p + 1 - 2 * odd

    loads = []
    for i, rows in enumerate(tiles(R)):
        c = pltpu.make_async_copy(x_hbm.at[rows], x.at[rows], load_sem.at[i])
        c.start()
        loads.append(c)
    barrier = pltpu.get_barrier_semaphore()
    for d in range(1, N):
        pl.semaphore_signal(
            barrier, inc=1, device_id={"row": lax.rem(r + d, N)}, device_id_type=MESH
        )
    for to in (slow, quick):
        pl.semaphore_signal(barrier, inc=1, device_id={"pair": to}, device_id_type=MESH)

    chunks = []
    for i, nb in enumerate(CHUNKS1 + CHUNKS2):
        chunks.append(
            Reduce(r, nb, *ar_bufs[3 * i : 3 * i + 3], ss.at[i], rs.at[i], sa.at[i], ra.at[i])
        )
    first, second = chunks[: len(CHUNKS1)], chunks[len(CHUNKS1) :]

    for i, rows in enumerate(tiles(R)):
        loads[i].wait()
        xv = x[rows, :]
        hi, lo = split(xv)
        xh[0, rows, :] = hi
        xh[1, rows, :] = lo
        xt[:, rows] = hi.astype(F32).T.astype(BF16)
    lead, trail = pl.ds(0, H), pl.ds(H, H)

    def mixed(i, j):
        return dot(xt[i, :], xh[1, :, j])

    def square(i, j):
        return dot(xt[i, :], xh[0, :, j])

    cross = square(lead, trail) + (mixed(lead, trail) + mixed(trail, lead).T)
    for j in range(4):
        i0, j0 = 128 * (j // 2), 128 * (j % 2)
        first[0].put(j, cross[i0 : i0 + 128, j0 : j0 + 128])
    pl.semaphore_wait(barrier, N + 1)
    first[0].scatter()
    for c, cols in ((1, lead), (2, trail)):
        m = mixed(cols, cols)
        g = square(cols, cols) + (m + m.T)
        first[c].put(0, g[:128, :128])
        first[c].put(1, g[:128, 128:])
        first[c].put(2, g[128:, 128:])
        first[c].scatter()
    for c in first:
        c.gather()

    sq = jnp.zeros((8, 128), F32)

    def norm(block, weight):
        return weight * jnp.sum((block * block).reshape(16, 8, 128), axis=0)

    first[0].arrive()
    for j in range(4):
        i0, j0 = 128 * (j // 2), 128 * (j % 2)
        b = first[0].get(j)
        sq = sq + norm(b, 2.0)
        a[i0 : i0 + 128, H + j0 : H + j0 + 128] = b
        a[H + j0 : H + j0 + 128, i0 : i0 + 128] = b.T
    for c, o in ((1, 0), (2, H)):
        first[c].arrive()
        b0, b1, b2 = (first[c].get(j) for j in range(3))
        sq = sq + norm(b0, 1.0) + norm(b1, 2.0) + norm(b2, 1.0)
        a[o : o + 128, o : o + 128] = b0
        a[o : o + 128, o + 128 : o + 256] = b1
        a[o + 128 : o + 256, o : o + 128] = b1.T
        a[o + 128 : o + 256, o + 128 : o + 256] = b2
    scale = jnp.sqrt(jnp.sum(sq, keepdims=True) + EPS)
    inv = 1.0 / scale
    for rows in tiles(W):
        a[rows, :] = a[rows, :] * inv
    newton_schulz(a, ah, a2, u, v, z2, z2h, yh, z)
    back = jnp.sqrt(ROWS / scale)

    lead_slow = (mv_ref[...] + odd) == 1
    for rows in tiles(W):
        zl, zt = z[rows, :H] * back, z[rows, H:] * back
        keep(u, rows, jnp.concatenate(
            [jnp.where(lead_slow, zl, zt), jnp.where(lead_slow, zt, zl)], axis=1))
        keep(z2h, rows, z[rows, :])

    def send(src, dst, i, to):
        c = pltpu.make_async_remote_copy(
            src_ref=src, dst_ref=dst, send_sem=xs.at[i], recv_sem=xr.at[i],
            device_id={"pair": to}, device_id_type=MESH,
        )
        c.start()
        return c

    for rows in tiles(R):
        t = product(xh, rows, u, lead)
        s_out[0, rows, :] = t[:, :128]
        s_out[1, rows, :] = t[:, 128:]
    s_sent = [send(s_out.at[c], s_in.at[c], c, slow) for c in range(2)]
    for rows in tiles(R):
        q_out[rows, :] = product(xh, rows, u, trail)
    q_sent = send(q_out, q_in, 2, quick)

    for rows in tiles(W):
        keep(v, rows, product(z2h, rows, ah))
    dl, dt = product(z2h, lead, v, lead), product(z2h, trail, v, trail)
    d_out[0] = jnp.where(lead_slow, dl, dt) * float(ROWS)
    d_out[1] = jnp.where(lead_slow, dt, dl) * float(ROWS)
    d_sent = [send(d_out.at[i], d_in.at[i], 3 + i, to) for i, to in ((0, slow), (1, quick))]

    q_sent.wait_recv()
    for rows in tiles(R):
        hi, lo = split(q_in[rows, :])
        nh[0, rows, H:] = hi
        nh[1, rows, H:] = lo
        qt[0, :, rows] = hi.astype(F32).T.astype(BF16)
        qt[1, :, rows] = lo.astype(F32).T.astype(BF16)
    for c in range(2):
        cols = pl.ds(128 * c, 128)
        s_sent[c].wait_recv()
        for rows in tiles(R):
            hi, lo = split(s_in[c, rows, :])
            nh[0, rows, cols] = hi
            nh[1, rows, cols] = lo
        g = dot(qt[0], nh[0, :, cols]) + (dot(qt[0], nh[1, :, cols]) + dot(qt[1], nh[0, :, cols]))
        second[c].put(0, g[:128])
        second[c].put(1, g[128:])
        second[c].scatter()
    for c in second:
        c.gather()
    for c in d_sent:
        c.wait_recv()
    sq = jnp.zeros((8, 128), F32)
    for i, o in ((0, 0), (1, H)):
        for rows in range(0, H, 128):
            b = d_in[i, rows : rows + 128, :]
            sq = sq + norm(b[:, :128], 1.0) + norm(b[:, 128:], 1.0)
            a[o + rows : o + rows + 128, o : o + H] = b
    for c in range(2):
        second[c].arrive()
        for j in range(2):
            b = second[c].get(j)
            sq = sq + norm(b, 2.0)
            i0, j0 = H + 128 * j, 128 * c
            a[i0 : i0 + 128, j0 : j0 + 128] = b
            a[j0 : j0 + 128, i0 : i0 + 128] = b.T
    scale = jnp.sqrt(jnp.sum(sq, keepdims=True) + EPS)
    inv = 1.0 / scale
    for rows in tiles(W):
        a[rows, :] = a[rows, :] * inv
    newton_schulz(a, ah, a2, u, v, z2, z2h, yh, z)
    back = jnp.sqrt(ROWS / scale)
    for rows in tiles(W):
        keep(u, rows, z[rows, :] * back)
    s_cols = pl.ds(pl.multiple_of(odd * H, H), H)
    q_cols = pl.ds(pl.multiple_of((1 - odd) * H, H), H)
    stores = []
    for i, rows in enumerate(tiles(R)):
        t = product(nh, rows, u)
        out[0, rows, :] = t[:, :H]
        out[1, rows, :] = t[:, H:]
        for k, cols in ((0, s_cols), (1, q_cols)):
            c = pltpu.make_async_copy(
                out.at[k, rows], out_hbm.at[rows, cols], out_sem.at[2 * i + k]
            )
            c.start()
            stores.append(c)
    for c in s_sent + [q_sent] + d_sent:
        c.wait_send()
    for c in chunks:
        c.drain()
    for c in stores:
        c.wait()


def local(slab, moves):
    ar = []
    for nb in CHUNKS1 + CHUNKS2:
        ar += [pltpu.VMEM((N, nb, 8, 128), F32)] * 3
    n_ar = len(CHUNKS1) + len(CHUNKS2)
    half = lambda *s: pltpu.VMEM(s, BF16)
    full = lambda *s: pltpu.VMEM(s, F32)
    return pl.pallas_call(
        kernel,
        out_shape=jax.ShapeDtypeStruct((R, W), F32),
        in_specs=[
            pl.BlockSpec(memory_space=pl.ANY),
            pl.BlockSpec(memory_space=pltpu.VMEM),
        ],
        out_specs=pl.BlockSpec(memory_space=pl.ANY),
        scratch_shapes=ar
        + [
            full(R, W), half(2, R, W), half(W, R),
            full(W, W), half(2, W, W), full(W, W), half(2, W, W), half(2, W, W),
            full(W, W), half(2, W, W), half(2, W, W), full(W, W),
            full(2, H, H), full(2, H, H),
            full(2, R, 128), full(2, R, 128), full(R, H), full(R, H),
            half(2, R, W), half(2, H, R), full(2, R, H),
            pltpu.SemaphoreType.DMA((4,)),
            pltpu.SemaphoreType.DMA((8,)),
            pltpu.SemaphoreType.DMA((n_ar,)),
            pltpu.SemaphoreType.DMA((n_ar,)),
            pltpu.SemaphoreType.DMA((n_ar,)),
            pltpu.SemaphoreType.DMA((n_ar,)),
            pltpu.SemaphoreType.DMA((5,)),
            pltpu.SemaphoreType.DMA((5,)),
        ],
        compiler_params=pltpu.CompilerParams(
            collective_id=1, has_side_effects=True, vmem_limit_bytes=50 * 2**20
        ),
    )(slab, moves)


def solution(mesh):
    placed = (P("row", "pair"), P(None, "pair"))
    return jax.shard_map(
        local, mesh=mesh, in_specs=placed, out_specs=P("row", "pair"), check_vma=False
    )
```

time: 375 us -> 83 us (0.22)
  waiting for transfers between devices: 293 us -> 0 us
  Pallas kernels: 0 us -> 80.9 us
  matrix products: 49 us -> 0 us
  between operations: 16 us -> 0.66 us
  starting transfers between devices: 5.91 us -> 0 us
  other arithmetic: 4.49 us -> 0 us
    psum x2 -> x0, waiting for transfers between devices: 281 us -> none  [local(): gram_whole = lax.psum(partial_value, 'row')]
    pallas_call x0 -> x1, Pallas kernels: none -> 80.9 us  [local(): pl.pallas_call(kernel, out_shape=jax.ShapeDtypeStruct((R, W), F32), in_sp...]
    dot_general x16 -> x0, matrix products: 49 us -> none  [the longest x14 40 us: product(): jnp.dot(left_side, right_side, precision=lax.Precision.HIGHEST, preferred...]
    ppermute x2 -> x0, waiting for transfers between devices: 12.3 us -> none  [from_behind(): return lax.ppermute(block, axis, route)]
    ppermute x2 -> x0, starting transfers between devices: 5.58 us -> none  [from_behind(): return lax.ppermute(block, axis, route)]
    reduce_sum x2 -> x0, other arithmetic: 4.2 us -> none  [inverse_full(): gram_scale = jnp.sqrt(jnp.sum(gram_full * gram_full) + epsilon)]
  transfers between devices with their start and end apart: 4 -> 0, of which waited for: 3 -> 0; matrix products, arithmetic and copies ran while one was open for 0% -> 0% of each run, Pallas kernels for 0% -> 0%
where the time goes in v1:
time: 83 us; the launch traced here: 82.9 us
  Pallas kernels  80.9 us (97%)
  local copies, waits for them, and re-layouts  1.32 us (2%)
    pallas_call x1, Pallas kernels, local(): pl.pallas_call(kernel, out_shape=jax.ShapeDtypeStruct((R, W), F32), in_sp...  80.9 us

profile of v1, /device:TPU:8, one launch (start us, length us, event | category | flops | bytes accessed | tf_op | source)
XLA Modules:
  0.0 82.9 jit_solution(2464060645953105085)
XLA Ops:
  0.7 80.9 %shard_map.28 = f32[1024,512]{1,0:T(8,128)S(1)} custom-call(f32[1024,512]{1,0:T(8,128)} %x_hbm.1, s32[1,1]{1,0:T(1,128)S(6)} %copy.4.mv_ref), custom_call_target="tpu_custom_call" | custom-call | tf_op jit(solution)/shard_map/pallas_call | solution.py:330
  81.5 1.3 %copy.5 = f32[1024,512]{1,0:T(8,128)} copy(f32[1024,512]{1,0:T(8,128)S(1)} %shard_map.28) | data formatting | bytes 4194304

commit v2 on v1

--- a/solution.py
+++ b/solution.py
@@ -17,7 +17,7 @@
 ROWS = 16384
 EPS = 1e-06
 T = 256
-CHUNKS1 = (4, 3, 3)
+CHUNKS1 = ((2, 0), (2, 0), (2, 0), (2, 2))
 CHUNKS2 = (2, 2)
 
 
@@ -52,25 +52,28 @@
     return jnp.where(r == c, 1.0, 0.0).astype(F32)
 
 
-def newton_schulz(a, ah, a2, u, v, z2, z2h, yh, z):
+def symmetric(a, b):
+    top = product(a, pl.ds(0, H), b)
+    low = product(a, pl.ds(H, H), b, pl.ds(H, H))
+    return top, jnp.concatenate([top[:, H:].T, low], axis=1)
+
+
+def newton_schulz(a, ah, a2, u, v, z2, z2h, yh):
     for rows in tiles(W):
         keep(ah, rows, a[rows, :])
-    for rows in tiles(W):
+    for rows, sq in zip(tiles(W), symmetric(ah, ah)):
         at = a[rows, :]
-        sq = product(ah, rows, ah)
         a2[rows, :] = sq
         keep(u, rows, sq - 5.0 * at)
         keep(v, rows, sq - 4.0 * at)
-    for i, rows in enumerate(tiles(W)):
-        p = product(u, rows, v)
+    for i, (rows, p) in enumerate(zip(tiles(W), symmetric(u, v))):
         t = (p + 7.0 * a2[rows, :] - 39.0 * a[rows, :] + 36.0 * eye_tile(i)) * 0.0625
         z2[rows, :] = t
         keep(z2h, rows, t)
-    for rows in tiles(W):
-        keep(yh, rows, product(z2h, rows, ah))
-        keep(u, rows, product(z2h, rows, z2h))
-    for rows in tiles(W):
-        z[rows, :] = 1.5 * z2[rows, :] - 0.5 * product(u, rows, yh)
+    for rows, y in zip(tiles(W), symmetric(z2h, ah)):
+        keep(yh, rows, y)
+    for rows, t in zip(tiles(W), symmetric(z2h, z2h)):
+        keep(u, rows, t)
 
 
 class Reduce:
@@ -132,19 +135,112 @@
         self._all(self.whole, self.whole, self.sa, self.ra).wait_send()
 
 
+class Fold:
+    def __init__(self, r, nb, part, yb, half, zb, whole, ss, rs):
+        self.r, self.z, self.y = r, r // 2, lax.rem(r, 2)
+        self.other = r + 1 - 2 * self.y
+        self.nb = nb
+        self.part, self.yb, self.half, self.zb, self.whole = part, yb, half, zb, whole
+        self.ss, self.rs = ss, rs
+
+    def put(self, j, block):
+        self.part[:, :, 8 * j : 8 * j + 8, :] = block.reshape(2, 8, 8, 128)
+
+    def put_rows(self, rows):
+        at = 8 * self.nb
+        self.part[:, :, at : at + 2, :] = jnp.zeros((2, 8, 2, 128), F32)
+        self.part[0, 0, at : at + 2, :] = rows
+
+    def copy(self, src, dst, i, row):
+        return pltpu.make_async_remote_copy(
+            src_ref=src, dst_ref=dst, send_sem=self.ss.at[i], recv_sem=self.rs.at[i],
+            device_id={"row": row}, device_id_type=MESH,
+        )
+
+    def over_y(self):
+        return self.copy(self.part.at[1 - self.y], self.yb, 0, self.other)
+
+    def seven(self, i):
+        return self.copy(self.half.at[pl.ds(1, 7)], self.zb.at[pl.ds(1, 7)], i, self.other)
+
+    def back_y(self):
+        mine = self.whole.at[self.y]
+        return self.copy(mine, mine, 3, self.other)
+
+    def scatter_y(self):
+        self.over_y().start()
+
+    def scatter_z(self):
+        self.over_y().wait_recv()
+        self.half[...] = self.part[self.y] + self.yb[...]
+        for d in ORDER_Z:
+            to = lax.rem(self.z + d, 8)
+            self.copy(self.half.at[to], self.zb.at[8 - d], 1, to * 2 + self.y).start()
+
+    def gather_z(self):
+        self.seven(1).wait_recv()
+        total = self.half[self.z]
+        for d in range(1, 8):
+            total = total + self.zb[d]
+        self.whole[self.y, self.z] = total
+        mine = self.whole.at[self.y, self.z]
+        for d in ORDER_Z:
+            self.copy(mine, mine, 2, lax.rem(self.z + d, 8) * 2 + self.y).start()
+
+    def gather_y(self):
+        self.seven(2).wait_recv()
+        self.back_y().start()
+
+    def arrive(self):
+        self.back_y().wait_recv()
+
+    def get(self, j):
+        return self.whole[:, :, 8 * j : 8 * j + 8, :].reshape(128, 128)
+
+    def get_row(self, k):
+        at = 8 * self.nb + k
+        return self.whole[0, 0, at : at + 1, :]
+
+    def drain(self):
+        self.over_y().wait_send()
+        self.seven(1).wait_send()
+        self.seven(2).wait_send()
+        self.back_y().wait_send()
+
+
+ORDER_Z = (4, 3, 5, 2, 6, 1, 7)
 ORDER = (8, 7, 9, 6, 10, 5, 11, 4, 12, 3, 13, 2, 14, 1, 15)
 
 
+def upper():
+    r = lax.broadcasted_iota(jnp.int32, (128, 128), 0)
+    c = lax.broadcasted_iota(jnp.int32, (128, 128), 1)
+    return r < c, r == c
+
+
+def norm(block, weight):
+    return weight * jnp.sum((block * block).reshape(-1, 8, block.shape[1]), axis=0)
+
+
 def kernel(x_hbm, mv_ref, out_hbm, *refs):
-    n_ar = len(CHUNKS1) + len(CHUNKS2)
-    ar_bufs, refs = refs[: 3 * n_ar], refs[3 * n_ar :]
-    (x, xh, xt, a, ah, a2, u, v, z2, z2h, yh, z, d_out, d_in,
+    n1, n2 = len(CHUNKS1), len(CHUNKS2)
+    bufs1, refs = refs[: 5 * n1], refs[5 * n1 :]
+    bufs2, refs = refs[: 3 * n2], refs[3 * n2 :]
+    (x, xh, xt, a, ah, a2, u, v, z2, z2h, yh, zh, d_out, d_in,
      s_out, s_in, q_out, q_in, nh, qt, out,
-     load_sem, out_sem, ss, rs, sa, ra, xs, xr) = refs
+     load_sem, out_sem, ss1, rs1, ss2, rs2, xs, xr) = refs
     r, p = lax.axis_index("row"), lax.axis_index("pair")
     odd = lax.rem(p, 2)
     slow = lax.rem(p + (N - 1) + 2 * odd, N)
     quick = p + 1 - 2 * odd
+    first = [
+        Fold(r, nb, *bufs1[5 * i : 5 * i + 5], ss1.at[i], rs1.at[i])
+        for i, (nb, _) in enumerate(CHUNKS1)
+    ]
+    second = [
+        Reduce(r, nb, *bufs2[3 * i : 3 * i + 3], ss2.at[2 * i], rs2.at[2 * i], ss2.at[2 * i + 1], rs2.at[2 * i + 1])
+        for i, nb in enumerate(CHUNKS2)
+    ]
 
     loads = []
     for i, rows in enumerate(tiles(R)):
@@ -159,21 +255,16 @@
     for to in (slow, quick):
         pl.semaphore_signal(barrier, inc=1, device_id={"pair": to}, device_id_type=MESH)
 
-    chunks = []
-    for i, nb in enumerate(CHUNKS1 + CHUNKS2):
-        chunks.append(
-            Reduce(r, nb, *ar_bufs[3 * i : 3 * i + 3], ss.at[i], rs.at[i], sa.at[i], ra.at[i])
-        )
-    first, second = chunks[: len(CHUNKS1)], chunks[len(CHUNKS1) :]
-
+    lead_slow = (mv_ref[...] + odd) == 1
     for i, rows in enumerate(tiles(R)):
         loads[i].wait()
-        xv = x[rows, :]
-        hi, lo = split(xv)
+        xl, xr_ = x[rows, :H], x[rows, H:]
+        hi, lo = split(jnp.concatenate(
+            [jnp.where(lead_slow, xl, xr_), jnp.where(lead_slow, xr_, xl)], axis=1))
         xh[0, rows, :] = hi
         xh[1, rows, :] = lo
         xt[:, rows] = hi.astype(F32).T.astype(BF16)
-    lead, trail = pl.ds(0, H), pl.ds(H, H)
+    sc, qc = pl.ds(0, H), pl.ds(H, H)
 
     def mixed(i, j):
         return dot(xt[i, :], xh[1, :, j])
@@ -181,55 +272,62 @@
     def square(i, j):
         return dot(xt[i, :], xh[0, :, j])
 
-    cross = square(lead, trail) + (mixed(lead, trail) + mixed(trail, lead).T)
+    cross = square(sc, qc) + (mixed(sc, qc) + mixed(qc, sc).T)
     for j in range(4):
         i0, j0 = 128 * (j // 2), 128 * (j % 2)
-        first[0].put(j, cross[i0 : i0 + 128, j0 : j0 + 128])
+        first[j // 2].put(j % 2, cross[i0 : i0 + 128, j0 : j0 + 128])
     pl.semaphore_wait(barrier, N + 1)
-    first[0].scatter()
-    for c, cols in ((1, lead), (2, trail)):
+    first[0].scatter_y()
+    first[1].scatter_y()
+    above, on = upper()
+    packed, diagonal = [], []
+    for c, cols in enumerate((sc, qc)):
         m = mixed(cols, cols)
         g = square(cols, cols) + (m + m.T)
-        first[c].put(0, g[:128, :128])
-        first[c].put(1, g[:128, 128:])
-        first[c].put(2, g[128:, 128:])
-        first[c].scatter()
+        first[2].put(c, g[:128, 128:])
+        low = g[128:, 128:]
+        first[3].put(c, jnp.where(above | on, g[:128, :128], low))
+        diagonal.append(jnp.sum(jnp.where(on, low, 0.0), axis=0, keepdims=True))
+    first[3].put_rows(jnp.concatenate(diagonal, axis=0))
+    first[2].scatter_y()
+    first[3].scatter_y()
     for c in first:
-        c.gather()
+        c.scatter_z()
+    for c in first:
+        c.gather_z()
+    for c in first:
+        c.gather_y()
 
     sq = jnp.zeros((8, 128), F32)
-
-    def norm(block, weight):
-        return weight * jnp.sum((block * block).reshape(16, 8, 128), axis=0)
-
-    first[0].arrive()
     for j in range(4):
+        if j % 2 == 0:
+            first[j // 2].arrive()
         i0, j0 = 128 * (j // 2), 128 * (j % 2)
-        b = first[0].get(j)
+        b = first[j // 2].get(j % 2)
         sq = sq + norm(b, 2.0)
         a[i0 : i0 + 128, H + j0 : H + j0 + 128] = b
         a[H + j0 : H + j0 + 128, i0 : i0 + 128] = b.T
-    for c, o in ((1, 0), (2, H)):
-        first[c].arrive()
-        b0, b1, b2 = (first[c].get(j) for j in range(3))
-        sq = sq + norm(b0, 1.0) + norm(b1, 2.0) + norm(b2, 1.0)
+    first[2].arrive()
+    for c, o in ((0, 0), (1, H)):
+        b = first[2].get(c)
+        sq = sq + norm(b, 2.0)
+        a[o : o + 128, o + 128 : o + 256] = b
+        a[o + 128 : o + 256, o : o + 128] = b.T
+    first[3].arrive()
+    for c, o in ((0, 0), (1, H)):
+        b = first[3].get(c)
+        t = b.T
+        b0 = jnp.where(above | on, b, t)
+        b2 = jnp.where(above, t, jnp.where(on, first[3].get_row(c), b))
+        sq = sq + norm(b0, 1.0) + norm(b2, 1.0)
         a[o : o + 128, o : o + 128] = b0
-        a[o : o + 128, o + 128 : o + 256] = b1
-        a[o + 128 : o + 256, o : o + 128] = b1.T
         a[o + 128 : o + 256, o + 128 : o + 256] = b2
     scale = jnp.sqrt(jnp.sum(sq, keepdims=True) + EPS)
     inv = 1.0 / scale
     for rows in tiles(W):
         a[rows, :] = a[rows, :] * inv
-    newton_schulz(a, ah, a2, u, v, z2, z2h, yh, z)
+    newton_schulz(a, ah, a2, u, v, z2, z2h, yh)
     back = jnp.sqrt(ROWS / scale)
-
-    lead_slow = (mv_ref[...] + odd) == 1
-    for rows in tiles(W):
-        zl, zt = z[rows, :H] * back, z[rows, H:] * back
-        keep(u, rows, jnp.concatenate(
-            [jnp.where(lead_slow, zl, zt), jnp.where(lead_slow, zt, zl)], axis=1))
-        keep(z2h, rows, z[rows, :])
 
     def send(src, dst, i, to):
         c = pltpu.make_async_remote_copy(
@@ -239,21 +337,36 @@
         c.start()
         return c
 
-    for rows in tiles(R):
-        t = product(xh, rows, u, lead)
+    top = 1.5 * z2[sc, :] - 0.5 * product(u, sc, yh)
+    left = top[:, H:].T
+    hi, lo = split(top[:, :H] * back)
+    zh[0, sc, sc], zh[1, sc, sc] = hi, lo
+    hi, lo = split(left * back)
+    zh[0, qc, sc], zh[1, qc, sc] = hi, lo
+    s_sent = [[], []]
+    for i, rows in enumerate(tiles(R)):
+        t = product(xh, rows, zh, sc)
         s_out[0, rows, :] = t[:, :128]
         s_out[1, rows, :] = t[:, 128:]
-    s_sent = [send(s_out.at[c], s_in.at[c], c, slow) for c in range(2)]
+        s_sent[0].append(send(s_out.at[0, rows], s_in.at[0, rows], i, slow))
+    for i, rows in enumerate(tiles(R)):
+        s_sent[1].append(send(s_out.at[1, rows], s_in.at[1, rows], 4 + i, slow))
+    low = 1.5 * z2[qc, qc] - 0.5 * product(u, qc, yh, qc)
+    hi, lo = split(top[:, H:] * back)
+    zh[0, sc, qc], zh[1, sc, qc] = hi, lo
+    hi, lo = split(low * back)
+    zh[0, qc, qc], zh[1, qc, qc] = hi, lo
     for rows in tiles(R):
-        q_out[rows, :] = product(xh, rows, u, trail)
-    q_sent = send(q_out, q_in, 2, quick)
-
-    for rows in tiles(W):
-        keep(v, rows, product(z2h, rows, ah))
-    dl, dt = product(z2h, lead, v, lead), product(z2h, trail, v, trail)
-    d_out[0] = jnp.where(lead_slow, dl, dt) * float(ROWS)
-    d_out[1] = jnp.where(lead_slow, dt, dl) * float(ROWS)
-    d_sent = [send(d_out.at[i], d_in.at[i], 3 + i, to) for i, to in ((0, slow), (1, quick))]
+        q_out[rows, :] = product(xh, rows, zh, qc)
+    q_sent = send(q_out, q_in, 8, quick)
+
+    keep(z2h, sc, top)
+    keep(z2h, qc, jnp.concatenate([left, low], axis=1))
+    for rows, t in zip(tiles(W), symmetric(z2h, ah)):
+        keep(v, rows, t)
+    d_out[0] = product(z2h, sc, v, sc) * float(ROWS)
+    d_out[1] = product(z2h, qc, v, qc) * float(ROWS)
+    d_sent = [send(d_out.at[i], d_in.at[i], 9 + i, to) for i, to in ((0, slow), (1, quick))]
 
     q_sent.wait_recv()
     for rows in tiles(R):
@@ -264,8 +377,8 @@
         qt[1, :, rows] = lo.astype(F32).T.astype(BF16)
     for c in range(2):
         cols = pl.ds(128 * c, 128)
-        s_sent[c].wait_recv()
-        for rows in tiles(R):
+        for i, rows in enumerate(tiles(R)):
+            s_sent[c][i].wait_recv()
             hi, lo = split(s_in[c, rows, :])
             nh[0, rows, cols] = hi
             nh[1, rows, cols] = lo
@@ -295,15 +408,17 @@
     inv = 1.0 / scale
     for rows in tiles(W):
         a[rows, :] = a[rows, :] * inv
-    newton_schulz(a, ah, a2, u, v, z2, z2h, yh, z)
+    newton_schulz(a, ah, a2, u, v, z2, z2h, yh)
     back = jnp.sqrt(ROWS / scale)
-    for rows in tiles(W):
-        keep(u, rows, z[rows, :] * back)
+    top = (1.5 * z2[sc, :] - 0.5 * product(u, sc, yh)) * back
+    low = (1.5 * z2[qc, qc] - 0.5 * product(u, qc, yh, qc)) * back
+    keep(zh, sc, top)
+    keep(zh, qc, jnp.concatenate([top[:, H:].T, low], axis=1))
     s_cols = pl.ds(pl.multiple_of(odd * H, H), H)
     q_cols = pl.ds(pl.multiple_of((1 - odd) * H, H), H)
     stores = []
     for i, rows in enumerate(tiles(R)):
-        t = product(nh, rows, u)
+        t = product(nh, rows, zh)
         out[0, rows, :] = t[:, :H]
         out[1, rows, :] = t[:, H:]
         for k, cols in ((0, s_cols), (1, q_cols)):
@@ -312,21 +427,25 @@
             )
             c.start()
             stores.append(c)
-    for c in s_sent + [q_sent] + d_sent:
+    for c in s_sent[0] + s_sent[1] + [q_sent] + d_sent:
         c.wait_send()
-    for c in chunks:
+    for c in first + second:
         c.drain()
     for c in stores:
         c.wait()
 
 
 def local(slab, moves):
-    ar = []
-    for nb in CHUNKS1 + CHUNKS2:
-        ar += [pltpu.VMEM((N, nb, 8, 128), F32)] * 3
-    n_ar = len(CHUNKS1) + len(CHUNKS2)
     half = lambda *s: pltpu.VMEM(s, BF16)
     full = lambda *s: pltpu.VMEM(s, F32)
+    bufs = []
+    for nb, more in CHUNKS1:
+        t = (8 * nb + more, 128)
+        bufs += [full(2, 8, *t), full(8, *t), full(8, *t), full(8, *t), full(2, 8, *t)]
+    for nb in CHUNKS2:
+        bufs += [full(N, nb, 8, 128)] * 3
+    dma = lambda *n: pltpu.SemaphoreType.DMA(n)
+    n1, n2 = len(CHUNKS1), len(CHUNKS2)
     return pl.pallas_call(
         kernel,
         out_shape=jax.ShapeDtypeStruct((R, W), F32),
@@ -335,22 +454,15 @@
             pl.BlockSpec(memory_space=pltpu.VMEM),
         ],
         out_specs=pl.BlockSpec(memory_space=pl.ANY),
-        scratch_shapes=ar
+        scratch_shapes=bufs
         + [
             full(R, W), half(2, R, W), half(W, R),
             full(W, W), half(2, W, W), full(W, W), half(2, W, W), half(2, W, W),
-            full(W, W), half(2, W, W), half(2, W, W), full(W, W),
+            full(W, W), half(2, W, W), half(2, W, W), half(2, W, W),
             full(2, H, H), full(2, H, H),
             full(2, R, 128), full(2, R, 128), full(R, H), full(R, H),
             half(2, R, W), half(2, H, R), full(2, R, H),
-            pltpu.SemaphoreType.DMA((4,)),
-            pltpu.SemaphoreType.DMA((8,)),
-            pltpu.SemaphoreType.DMA((n_ar,)),
-            pltpu.SemaphoreType.DMA((n_ar,)),
-            pltpu.SemaphoreType.DMA((n_ar,)),
-            pltpu.SemaphoreType.DMA((n_ar,)),
-            pltpu.SemaphoreType.DMA((5,)),
-            pltpu.SemaphoreType.DMA((5,)),
+            dma(4), dma(8), dma(n1, 4), dma(n1, 4), dma(2 * n2), dma(2 * n2), dma(11), dma(11),
         ],
         compiler_params=pltpu.CompilerParams(
             collective_id=1, has_side_effects=True, vmem_limit_bytes=50 * 2**20

time: 83 us -> 73.1 us (0.88)
  Pallas kernels: 80.9 us -> 71 us
    pallas_call x1, Pallas kernels: 80.9 us -> 71 us  [local(): pl.pallas_call(kernel, out_shape=jax.ShapeDtypeStruct((R, W), F32), in_sp...]
where the time goes in v2:
time: 73.1 us; the launch traced here: 73 us
  Pallas kernels  71 us (97%)
  local copies, waits for them, and re-layouts  1.32 us (2%)
    pallas_call x1, Pallas kernels, local(): pl.pallas_call(kernel, out_shape=jax.ShapeDtypeStruct((R, W), F32), in_sp...  71 us

profile of v2, /device:TPU:8, one launch (start us, length us, event | category | flops | bytes accessed | tf_op | source)
XLA Modules:
  0.0 73.0 jit_solution(229827618540460563)
XLA Ops:
  0.7 71.0 %shard_map.28 = f32[1024,512]{1,0:T(8,128)S(1)} custom-call(f32[1024,512]{1,0:T(8,128)} %x_hbm.1, s32[1,1]{1,0:T(1,128)S(6)} %copy.4.mv_ref), custom_call_target="tpu_custom_call" | custom-call | tf_op jit(solution)/shard_map/pallas_call | solution.py:449
  71.7 1.3 %copy.5 = f32[1024,512]{1,0:T(8,128)} copy(f32[1024,512]{1,0:T(8,128)S(1)} %shard_map.28) | data formatting | bytes 4194304

commit v3 on v2

--- a/solution.py
+++ b/solution.py
@@ -18,7 +18,7 @@
 EPS = 1e-06
 T = 256
 CHUNKS1 = ((2, 0), (2, 0), (2, 0), (2, 2))
-CHUNKS2 = (2, 2)
+CHUNKS2 = (2, 1, 1)
 
 
 def dot(a, b):
@@ -30,10 +30,10 @@
     return hi, (v - hi.astype(F32)).astype(BF16)
 
 
-def keep(ref, rows, v):
+def keep(ref, rows, v, cols=slice(None)):
     hi, lo = split(v)
-    ref[0, rows, :] = hi
-    ref[1, rows, :] = lo
+    ref[0, rows, cols] = hi
+    ref[1, rows, cols] = lo
 
 
 def product(a, rows, b, cols=slice(None)):
@@ -58,11 +58,14 @@
     return top, jnp.concatenate([top[:, H:].T, low], axis=1)
 
 
-def newton_schulz(a, ah, a2, u, v, z2, z2h, yh):
+def newton_schulz(a, ah, inv, a2, u, v, z2, z2h, yh):
     for rows in tiles(W):
         keep(ah, rows, a[rows, :])
+    inv2 = inv * inv
     for rows, sq in zip(tiles(W), symmetric(ah, ah)):
-        at = a[rows, :]
+        at = a[rows, :] * inv
+        a[rows, :] = at
+        sq = sq * inv2
         a2[rows, :] = sq
         keep(u, rows, sq - 5.0 * at)
         keep(v, rows, sq - 4.0 * at)
@@ -71,68 +74,63 @@
         z2[rows, :] = t
         keep(z2h, rows, t)
     for rows, y in zip(tiles(W), symmetric(z2h, ah)):
-        keep(yh, rows, y)
+        keep(yh, rows, y * inv)
     for rows, t in zip(tiles(W), symmetric(z2h, z2h)):
         keep(u, rows, t)
 
 
-class Reduce:
-    def __init__(self, r, nb, part, parts, whole, ss, rs, sa, ra):
-        self.r, self.nb = r, nb
-        self.part, self.parts, self.whole = part, parts, whole
-        self.ss, self.rs, self.sa, self.ra = ss, rs, sa, ra
+class Line:
+    def __init__(self, r, nb, part, parts, mine, theirs, whole, ss, rs):
+        self.r, self.z, self.y = r, r // 2, lax.rem(r, 2)
+        self.other = r + 1 - 2 * self.y
+        self.part, self.parts, self.mine, self.theirs, self.whole = part, parts, mine, theirs, whole
+        self.ss, self.rs = ss, rs
 
     def put(self, j, block):
-        self.part[:, j] = block.reshape(N, 8, 128)
+        self.part[:, j] = block.reshape(8, 16, 128)
+
+    def copy(self, src, dst, i, row):
+        return pltpu.make_async_remote_copy(
+            src_ref=src, dst_ref=dst, send_sem=self.ss.at[i], recv_sem=self.rs.at[i],
+            device_id={"row": row}, device_id_type=MESH,
+        )
+
+    def seven(self, i):
+        return self.copy(self.part.at[pl.ds(1, 7)], self.parts.at[pl.ds(1, 7)], i, self.other)
+
+    def over_y(self):
+        return self.copy(self.mine, self.theirs, 1, self.other)
 
     def scatter(self):
-        for d in ORDER:
-            to = lax.rem(self.r + d, N)
-            pltpu.make_async_remote_copy(
-                src_ref=self.part.at[to],
-                dst_ref=self.parts.at[N - d],
-                send_sem=self.ss,
-                recv_sem=self.rs,
-                device_id={"row": to},
-                device_id_type=MESH,
-            ).start()
-
-    def _all(self, src, dst, ss, rs):
-        return pltpu.make_async_remote_copy(
-            src_ref=src.at[pl.ds(1, N - 1)],
-            dst_ref=dst.at[pl.ds(1, N - 1)],
-            send_sem=ss,
-            recv_sem=rs,
-            device_id={"row": lax.rem(self.r + 1, N)},
-            device_id_type=MESH,
-        )
+        for d in ORDER_Z:
+            to = lax.rem(self.z + d, 8)
+            self.copy(self.part.at[to], self.parts.at[8 - d], 0, to * 2 + self.y).start()
+
+    def swap(self):
+        self.seven(0).wait_recv()
+        total = self.part[self.z]
+        for d in range(1, 8):
+            total = total + self.parts[d]
+        self.mine[...] = total
+        self.over_y().start()
 
     def gather(self):
-        self._all(self.part, self.parts, self.ss, self.rs).wait_recv()
-        total = self.part[self.r]
-        for d in range(1, N):
-            total = total + self.parts[d]
-        self.whole[self.r] = total
-        for d in ORDER:
-            to = lax.rem(self.r + d, N)
-            pltpu.make_async_remote_copy(
-                src_ref=self.whole.at[self.r],
-                dst_ref=self.whole.at[self.r],
-                send_sem=self.sa,
-                recv_sem=self.ra,
-                device_id={"row": to},
-                device_id_type=MESH,
-            ).start()
+        self.over_y().wait_recv()
+        self.whole[self.z] = self.mine[...] + self.theirs[...]
+        mine = self.whole.at[self.z]
+        for d in ORDER_Z:
+            self.copy(mine, mine, 2, lax.rem(self.z + d, 8) * 2 + self.y).start()
 
     def arrive(self):
-        self._all(self.whole, self.whole, self.sa, self.ra).wait_recv()
+        self.seven(2).wait_recv()
 
     def get(self, j):
         return self.whole[:, j].reshape(128, 128)
 
     def drain(self):
-        self._all(self.part, self.parts, self.ss, self.rs).wait_send()
-        self._all(self.whole, self.whole, self.sa, self.ra).wait_send()
+        self.seven(0).wait_send()
+        self.over_y().wait_send()
+        self.seven(2).wait_send()
 
 
 class Fold:
@@ -209,26 +207,31 @@
 
 
 ORDER_Z = (4, 3, 5, 2, 6, 1, 7)
-ORDER = (8, 7, 9, 6, 10, 5, 11, 4, 12, 3, 13, 2, 14, 1, 15)
-
-
 def upper():
     r = lax.broadcasted_iota(jnp.int32, (128, 128), 0)
     c = lax.broadcasted_iota(jnp.int32, (128, 128), 1)
     return r < c, r == c
 
 
+def swap_halves(x):
+    return pltpu.roll(x, 64, 1)
+
+
+def beside(x, y):
+    return jnp.where(lax.broadcasted_iota(jnp.int32, x.shape, 1) < 64, x, y)
+
+
 def norm(block, weight):
     return weight * jnp.sum((block * block).reshape(-1, 8, block.shape[1]), axis=0)
 
 
-def kernel(x_hbm, mv_ref, out_hbm, *refs):
+def kernel(x_hbm, mv_ref, nh, zn, *refs):
     n1, n2 = len(CHUNKS1), len(CHUNKS2)
     bufs1, refs = refs[: 5 * n1], refs[5 * n1 :]
-    bufs2, refs = refs[: 3 * n2], refs[3 * n2 :]
+    bufs2, refs = refs[: 5 * n2], refs[5 * n2 :]
     (x, xh, xt, a, ah, a2, u, v, z2, z2h, yh, zh, d_out, d_in,
-     s_out, s_in, q_out, q_in, nh, qt, out,
-     load_sem, out_sem, ss1, rs1, ss2, rs2, xs, xr) = refs
+     s_out, s_in, p_out, p_in, q_out, q_in, qt,
+     load_sem, ss1, rs1, ss2, rs2, xs, xr) = refs
     r, p = lax.axis_index("row"), lax.axis_index("pair")
     odd = lax.rem(p, 2)
     slow = lax.rem(p + (N - 1) + 2 * odd, N)
@@ -238,7 +241,7 @@
         for i, (nb, _) in enumerate(CHUNKS1)
     ]
     second = [
-        Reduce(r, nb, *bufs2[3 * i : 3 * i + 3], ss2.at[2 * i], rs2.at[2 * i], ss2.at[2 * i + 1], rs2.at[2 * i + 1])
+        Line(r, nb, *bufs2[5 * i : 5 * i + 5], ss2.at[i], rs2.at[i])
         for i, nb in enumerate(CHUNKS2)
     ]
 
@@ -324,9 +327,7 @@
         a[o + 128 : o + 256, o + 128 : o + 256] = b2
     scale = jnp.sqrt(jnp.sum(sq, keepdims=True) + EPS)
     inv = 1.0 / scale
-    for rows in tiles(W):
-        a[rows, :] = a[rows, :] * inv
-    newton_schulz(a, ah, a2, u, v, z2, z2h, yh)
+    newton_schulz(a, ah, inv, a2, u, v, z2, z2h, yh)
     back = jnp.sqrt(ROWS / scale)
 
     def send(src, dst, i, to):
@@ -343,14 +344,18 @@
     zh[0, sc, sc], zh[1, sc, sc] = hi, lo
     hi, lo = split(left * back)
     zh[0, qc, sc], zh[1, qc, sc] = hi, lo
-    s_sent = [[], []]
+    s_sent = []
+    rest = []
     for i, rows in enumerate(tiles(R)):
         t = product(xh, rows, zh, sc)
-        s_out[0, rows, :] = t[:, :128]
-        s_out[1, rows, :] = t[:, 128:]
-        s_sent[0].append(send(s_out.at[0, rows], s_in.at[0, rows], i, slow))
-    for i, rows in enumerate(tiles(R)):
-        s_sent[1].append(send(s_out.at[1, rows], s_in.at[1, rows], 4 + i, slow))
+        s_out[rows, :] = t[:, :128]
+        s_sent.append(send(s_out.at[rows], s_in.at[rows], i, slow))
+        rest.append(t[:, 128:])
+    for i, rows in enumerate(tiles(W)):
+        p_out[0, rows, :] = beside(rest[i], swap_halves(rest[i + 2]))
+        p_out[1, rows, :] = beside(swap_halves(rest[i]), rest[i + 2])
+    for c in range(2):
+        s_sent.append(send(p_out.at[c], p_in.at[c], 4 + c, slow))
     low = 1.5 * z2[qc, qc] - 0.5 * product(u, qc, yh, qc)
     hi, lo = split(top[:, H:] * back)
     zh[0, sc, qc], zh[1, sc, qc] = hi, lo
@@ -358,15 +363,15 @@
     zh[0, qc, qc], zh[1, qc, qc] = hi, lo
     for rows in tiles(R):
         q_out[rows, :] = product(xh, rows, zh, qc)
-    q_sent = send(q_out, q_in, 8, quick)
+    q_sent = send(q_out, q_in, 6, quick)
 
     keep(z2h, sc, top)
     keep(z2h, qc, jnp.concatenate([left, low], axis=1))
     for rows, t in zip(tiles(W), symmetric(z2h, ah)):
-        keep(v, rows, t)
+        keep(v, rows, t * inv)
     d_out[0] = product(z2h, sc, v, sc) * float(ROWS)
     d_out[1] = product(z2h, qc, v, qc) * float(ROWS)
-    d_sent = [send(d_out.at[i], d_in.at[i], 9 + i, to) for i, to in ((0, slow), (1, quick))]
+    d_sent = [send(d_out.at[i], d_in.at[i], 7 + i, to) for i, to in ((0, slow), (1, quick))]
 
     q_sent.wait_recv()
     for rows in tiles(R):
@@ -375,19 +380,35 @@
         nh[1, rows, H:] = lo
         qt[0, :, rows] = hi.astype(F32).T.astype(BF16)
         qt[1, :, rows] = lo.astype(F32).T.astype(BF16)
+    cols = pl.ds(0, 128)
+    for i, rows in enumerate(tiles(R)):
+        s_sent[i].wait_recv()
+        hi, lo = split(s_in[rows, :])
+        nh[0, rows, cols] = hi
+        nh[1, rows, cols] = lo
+    g = dot(qt[0], nh[0, :, cols]) + (dot(qt[0], nh[1, :, cols]) + dot(qt[1], nh[0, :, cols]))
+    second[0].put(0, g[:128])
+    second[0].put(1, g[128:])
+    second[0].scatter()
     for c in range(2):
-        cols = pl.ds(128 * c, 128)
-        for i, rows in enumerate(tiles(R)):
-            s_sent[c][i].wait_recv()
-            hi, lo = split(s_in[c, rows, :])
-            nh[0, rows, cols] = hi
-            nh[1, rows, cols] = lo
-        g = dot(qt[0], nh[0, :, cols]) + (dot(qt[0], nh[1, :, cols]) + dot(qt[1], nh[0, :, cols]))
-        second[c].put(0, g[:128])
-        second[c].put(1, g[128:])
-        second[c].scatter()
-    for c in second:
-        c.gather()
+        s_sent[4 + c].wait_recv()
+        hi, lo = split(p_in[c])
+        parts = []
+        for k in (pl.ds(0, W), pl.ds(W, W)):
+            parts.append(dot(qt[0, :, k], hi) + (dot(qt[0, :, k], lo) + dot(qt[1, :, k], hi)))
+        g = parts[0] + swap_halves(parts[1])
+        second[1 + c].put(0, beside(g[:128], swap_halves(g[128:])))
+        second[1 + c].scatter()
+    for i, rows in enumerate(tiles(W)):
+        p0, p1 = p_in[0, rows, :], p_in[1, rows, :]
+        keep(nh, rows, beside(p0, swap_halves(p1)), pl.ds(128, 128))
+        keep(nh, pl.ds(W + i * T, T), beside(swap_halves(p0), p1), pl.ds(128, 128))
+    second[0].swap()
+    second[1].swap()
+    second[0].gather()
+    second[1].gather()
+    second[2].swap()
+    second[2].gather()
     for c in d_sent:
         c.wait_recv()
     sq = jnp.zeros((8, 128), F32)
@@ -396,24 +417,35 @@
             b = d_in[i, rows : rows + 128, :]
             sq = sq + norm(b[:, :128], 1.0) + norm(b[:, 128:], 1.0)
             a[o + rows : o + rows + 128, o : o + H] = b
-    for c in range(2):
-        second[c].arrive()
-        for j in range(2):
-            b = second[c].get(j)
-            sq = sq + norm(b, 2.0)
-            i0, j0 = H + 128 * j, 128 * c
-            a[i0 : i0 + 128, j0 : j0 + 128] = b
-            a[j0 : j0 + 128, i0 : i0 + 128] = b.T
+    def place(j, c, b):
+        i0, j0 = H + 128 * j, 128 * c
+        a[i0 : i0 + 128, j0 : j0 + 128] = b
+        a[j0 : j0 + 128, i0 : i0 + 128] = b.T
+        return norm(b, 2.0)
+
+    second[0].arrive()
+    for j in range(2):
+        sq = sq + place(j, 0, second[0].get(j))
+    for c in second[1:]:
+        c.arrive()
+    b0, b1 = second[1].get(0), second[2].get(0)
+    sq = sq + place(0, 1, beside(b0, swap_halves(b1))) + place(1, 1, beside(swap_halves(b0), b1))
     scale = jnp.sqrt(jnp.sum(sq, keepdims=True) + EPS)
     inv = 1.0 / scale
-    for rows in tiles(W):
-        a[rows, :] = a[rows, :] * inv
-    newton_schulz(a, ah, a2, u, v, z2, z2h, yh)
+    newton_schulz(a, ah, inv, a2, u, v, z2, z2h, yh)
     back = jnp.sqrt(ROWS / scale)
     top = (1.5 * z2[sc, :] - 0.5 * product(u, sc, yh)) * back
     low = (1.5 * z2[qc, qc] - 0.5 * product(u, qc, yh, qc)) * back
-    keep(zh, sc, top)
-    keep(zh, qc, jnp.concatenate([top[:, H:].T, low], axis=1))
+    keep(zn, sc, top)
+    keep(zn, qc, jnp.concatenate([top[:, H:].T, low], axis=1))
+    for c in s_sent + [q_sent] + d_sent:
+        c.wait_send()
+    for c in first + second:
+        c.drain()
+
+
+def last(nh, zh, out_hbm, out, out_sem):
+    odd = lax.rem(lax.axis_index("pair"), 2)
     s_cols = pl.ds(pl.multiple_of(odd * H, H), H)
     q_cols = pl.ds(pl.multiple_of((1 - odd) * H, H), H)
     stores = []
@@ -427,10 +459,6 @@
             )
             c.start()
             stores.append(c)
-    for c in s_sent[0] + s_sent[1] + [q_sent] + d_sent:
-        c.wait_send()
-    for c in first + second:
-        c.drain()
     for c in stores:
         c.wait()
 
@@ -443,31 +471,41 @@
         t = (8 * nb + more, 128)
         bufs += [full(2, 8, *t), full(8, *t), full(8, *t), full(8, *t), full(2, 8, *t)]
     for nb in CHUNKS2:
-        bufs += [full(N, nb, 8, 128)] * 3
+        t = (nb, 16, 128)
+        bufs += [full(8, *t), full(8, *t), full(*t), full(*t), full(8, *t)]
     dma = lambda *n: pltpu.SemaphoreType.DMA(n)
     n1, n2 = len(CHUNKS1), len(CHUNKS2)
-    return pl.pallas_call(
+    vmem = pl.BlockSpec(memory_space=pltpu.VMEM)
+    new, root = pl.pallas_call(
         kernel,
-        out_shape=jax.ShapeDtypeStruct((R, W), F32),
-        in_specs=[
-            pl.BlockSpec(memory_space=pl.ANY),
-            pl.BlockSpec(memory_space=pltpu.VMEM),
+        out_shape=[
+            jax.ShapeDtypeStruct((2, R, W), BF16),
+            jax.ShapeDtypeStruct((2, W, W), BF16),
         ],
-        out_specs=pl.BlockSpec(memory_space=pl.ANY),
+        in_specs=[pl.BlockSpec(memory_space=pltpu.HBM), vmem],
+        out_specs=[vmem, vmem],
         scratch_shapes=bufs
         + [
             full(R, W), half(2, R, W), half(W, R),
             full(W, W), half(2, W, W), full(W, W), half(2, W, W), half(2, W, W),
             full(W, W), half(2, W, W), half(2, W, W), half(2, W, W),
             full(2, H, H), full(2, H, H),
-            full(2, R, 128), full(2, R, 128), full(R, H), full(R, H),
-            half(2, R, W), half(2, H, R), full(2, R, H),
-            dma(4), dma(8), dma(n1, 4), dma(n1, 4), dma(2 * n2), dma(2 * n2), dma(11), dma(11),
+            full(R, 128), full(R, 128), full(2, W, 128), full(2, W, 128), full(R, H), full(R, H),
+            half(2, H, R),
+            dma(4), dma(n1, 4), dma(n1, 4), dma(n2, 3), dma(n2, 3), dma(9), dma(9),
         ],
         compiler_params=pltpu.CompilerParams(
             collective_id=1, has_side_effects=True, vmem_limit_bytes=50 * 2**20
         ),
     )(slab, moves)
+    return pl.pallas_call(
+        last,
+        out_shape=jax.ShapeDtypeStruct((R, W), F32),
+        in_specs=[vmem, vmem],
+        out_specs=pl.BlockSpec(memory_space=pl.ANY),
+        scratch_shapes=[full(2, R, H), dma(8)],
+        compiler_params=pltpu.CompilerParams(vmem_limit_bytes=16 * 2**20),
+    )(new, root)
 
 
 def solution(mesh):

time: 73.1 us -> 71 us (0.971)
  local copies, waits for them, and re-layouts: 1.32 us -> 0 us
  Pallas kernels: 71 us -> 70.1 us
    unnamed x1 -> x0, local copies, waits for them, and re-layouts: 1.32 us -> none
    pallas_call x1 -> x2, Pallas kernels: 71 us -> 70.1 us  [the longest x1 67.4 us: local(): pl.pallas_call(kernel, out_shape=[jax.ShapeDtypeStruct((2, R, W), BF16),...]
where the time goes in v3:
time: 71 us; the launch traced here: 70.9 us
  Pallas kernels  70.1 us (99%)
  between operations  0.82 us (1%)
    pallas_call x1, Pallas kernels, local(): pl.pallas_call(kernel, out_shape=[jax.ShapeDtypeStruct((2, R, W), BF16),...  67.4 us
    pallas_call x1, Pallas kernels, local(): pl.pallas_call(last, out_shape=jax.ShapeDtypeStruct((R, W), F32), in_spec...  2.65 us

profile of v3, /device:TPU:8, one launch (start us, length us, event | category | flops | bytes accessed | tf_op | source)
XLA Modules:
  0.0 70.9 jit_solution(1890567109430549105)
XLA Ops:
  0.7 67.4 %shard_map.28 = (bf16[2,1024,512]{2,1,0:T(8,128)(2,1)S(1)}, bf16[2,512,512]{2,1,0:T(8,128)(2,1)S(1)}) custom-call(f32[1024,512]{1,0:T(8,128)} %x_hbm.1, s32[1,1]{1,0:T(1,128)S(6)} %copy.3.mv_ref), custom_call_target="tpu_custom_call" | custom-call | tf_op jit(solution)/shard_map/pallas_call | solution.py:479
  68.1 2.6 %shard_map.29 = f32[1024,512]{1,0:T(8,128)} custom-call(bf16[2,1024,512]{2,1,0:T(8,128)(2,1)S(1)} %get-tuple-element.7.nh, bf16[2,512,512]{2,1,0:T(8,128)(2,1)S(1)} %get-tuple-element.8.zh), custom_call_target="tpu_custom_call" | custom-call | tf_op jit(solution)/shard_map/pallas_call | solution.py:501

commit v4 on v3

--- a/solution.py
+++ b/solution.py
@@ -17,7 +17,8 @@
 ROWS = 16384
 EPS = 1e-06
 T = 256
-CHUNKS1 = ((2, 0), (2, 0), (2, 0), (2, 2))
+CHUNKS1 = ((2, 0), (2, 0), (2, 2))
+LINE1 = 2
 CHUNKS2 = (2, 1, 1)
 
 
@@ -39,7 +40,7 @@
 def product(a, rows, b, cols=slice(None)):
     ah, al = a[0, rows, :], a[1, rows, :]
     bh, bl = b[0, :, cols], b[1, :, cols]
-    return dot(ah, bh) + (dot(ah, bl) + dot(al, bh))
+    return dot(jnp.concatenate([ah, ah, al], axis=1), jnp.concatenate([bl, bh, bh], axis=0))
 
 
 def tiles(n):
@@ -67,10 +68,10 @@
         a[rows, :] = at
         sq = sq * inv2
         a2[rows, :] = sq
-        keep(u, rows, sq - 5.0 * at)
-        keep(v, rows, sq - 4.0 * at)
+        keep(u, rows, sq)
+        keep(v, rows, sq - 9.0 * at)
     for i, (rows, p) in enumerate(zip(tiles(W), symmetric(u, v))):
-        t = (p + 7.0 * a2[rows, :] - 39.0 * a[rows, :] + 36.0 * eye_tile(i)) * 0.0625
+        t = (p + 27.0 * a2[rows, :] - 39.0 * a[rows, :] + 36.0 * eye_tile(i)) * 0.0625
         z2[rows, :] = t
         keep(z2h, rows, t)
     for rows, y in zip(tiles(W), symmetric(z2h, ah)):
@@ -226,7 +227,7 @@
 
 
 def kernel(x_hbm, mv_ref, nh, zn, *refs):
-    n1, n2 = len(CHUNKS1), len(CHUNKS2)
+    n1, n2 = len(CHUNKS1), 1 + len(CHUNKS2)
     bufs1, refs = refs[: 5 * n1], refs[5 * n1 :]
     bufs2, refs = refs[: 5 * n2], refs[5 * n2 :]
     (x, xh, xt, a, ah, a2, u, v, z2, z2h, yh, zh, d_out, d_in,
@@ -240,10 +241,11 @@
         Fold(r, nb, *bufs1[5 * i : 5 * i + 5], ss1.at[i], rs1.at[i])
         for i, (nb, _) in enumerate(CHUNKS1)
     ]
-    second = [
+    lines = [
         Line(r, nb, *bufs2[5 * i : 5 * i + 5], ss2.at[i], rs2.at[i])
-        for i, nb in enumerate(CHUNKS2)
+        for i, nb in enumerate((LINE1, *CHUNKS2))
     ]
+    early, second = lines[0], lines[1:]
 
     loads = []
     for i, rows in enumerate(tiles(R)):
@@ -251,10 +253,9 @@
         c.start()
         loads.append(c)
     barrier = pltpu.get_barrier_semaphore()
-    for d in range(1, N):
-        pl.semaphore_signal(
-            barrier, inc=1, device_id={"row": lax.rem(r + d, N)}, device_id_type=MESH
-        )
+    z, y = r // 2, lax.rem(r, 2)
+    for row in [lax.rem(z + d, 8) * 2 + y for d in range(1, 8)] + [r + 1 - 2 * y]:
+        pl.semaphore_signal(barrier, inc=1, device_id={"row": row}, device_id_type=MESH)
     for to in (slow, quick):
         pl.semaphore_signal(barrier, inc=1, device_id={"pair": to}, device_id_type=MESH)
 
@@ -275,53 +276,59 @@
     def square(i, j):
         return dot(xt[i, :], xh[0, :, j])
 
-    cross = square(sc, qc) + (mixed(sc, qc) + mixed(qc, sc).T)
+    left = xt[sc, :]
+    cross = mixed(qc, sc).T + dot(
+        jnp.concatenate([left, left], axis=1), jnp.concatenate([xh[1, :, qc], xh[0, :, qc]], axis=0)
+    )
     for j in range(4):
         i0, j0 = 128 * (j // 2), 128 * (j % 2)
-        first[j // 2].put(j % 2, cross[i0 : i0 + 128, j0 : j0 + 128])
-    pl.semaphore_wait(barrier, N + 1)
+        (early if j < 2 else first[0]).put(j % 2, cross[i0 : i0 + 128, j0 : j0 + 128])
+    pl.semaphore_wait(barrier, 10)
     first[0].scatter_y()
-    first[1].scatter_y()
+    early.scatter()
     above, on = upper()
     packed, diagonal = [], []
     for c, cols in enumerate((sc, qc)):
         m = mixed(cols, cols)
         g = square(cols, cols) + (m + m.T)
-        first[2].put(c, g[:128, 128:])
+        first[1].put(c, g[:128, 128:])
         low = g[128:, 128:]
-        first[3].put(c, jnp.where(above | on, g[:128, :128], low))
+        first[2].put(c, jnp.where(above | on, g[:128, :128], low))
         diagonal.append(jnp.sum(jnp.where(on, low, 0.0), axis=0, keepdims=True))
-    first[3].put_rows(jnp.concatenate(diagonal, axis=0))
+    first[2].put_rows(jnp.concatenate(diagonal, axis=0))
+    first[1].scatter_y()
     first[2].scatter_y()
-    first[3].scatter_y()
     for c in first:
         c.scatter_z()
+    early.swap()
     for c in first:
         c.gather_z()
+    early.gather()
     for c in first:
         c.gather_y()
 
     sq = jnp.zeros((8, 128), F32)
     for j in range(4):
+        part = early if j < 2 else first[0]
         if j % 2 == 0:
-            first[j // 2].arrive()
+            part.arrive()
         i0, j0 = 128 * (j // 2), 128 * (j % 2)
-        b = first[j // 2].get(j % 2)
+        b = part.get(j % 2)
         sq = sq + norm(b, 2.0)
         a[i0 : i0 + 128, H + j0 : H + j0 + 128] = b
         a[H + j0 : H + j0 + 128, i0 : i0 + 128] = b.T
+    first[1].arrive()
+    for c, o in ((0, 0), (1, H)):
+        b = first[1].get(c)
+        sq = sq + norm(b, 2.0)
+        a[o : o + 128, o + 128 : o + 256] = b
+        a[o + 128 : o + 256, o : o + 128] = b.T
     first[2].arrive()
     for c, o in ((0, 0), (1, H)):
         b = first[2].get(c)
-        sq = sq + norm(b, 2.0)
-        a[o : o + 128, o + 128 : o + 256] = b
-        a[o + 128 : o + 256, o : o + 128] = b.T
-    first[3].arrive()
-    for c, o in ((0, 0), (1, H)):
-        b = first[3].get(c)
         t = b.T
         b0 = jnp.where(above | on, b, t)
-        b2 = jnp.where(above, t, jnp.where(on, first[3].get_row(c), b))
+        b2 = jnp.where(above, t, jnp.where(on, first[2].get_row(c), b))
         sq = sq + norm(b0, 1.0) + norm(b2, 1.0)
         a[o : o + 128, o : o + 128] = b0
         a[o + 128 : o + 256, o + 128 : o + 256] = b2
@@ -386,7 +393,10 @@
         hi, lo = split(s_in[rows, :])
         nh[0, rows, cols] = hi
         nh[1, rows, cols] = lo
-    g = dot(qt[0], nh[0, :, cols]) + (dot(qt[0], nh[1, :, cols]) + dot(qt[1], nh[0, :, cols]))
+    g = dot(
+        jnp.concatenate([qt[0], qt[0], qt[1]], axis=1),
+        jnp.concatenate([nh[1, :, cols], nh[0, :, cols], nh[0, :, cols]], axis=0),
+    )
     second[0].put(0, g[:128])
     second[0].put(1, g[128:])
     second[0].scatter()
@@ -395,7 +405,10 @@
         hi, lo = split(p_in[c])
         parts = []
         for k in (pl.ds(0, W), pl.ds(W, W)):
-            parts.append(dot(qt[0, :, k], hi) + (dot(qt[0, :, k], lo) + dot(qt[1, :, k], hi)))
+            qh = qt[0, :, k]
+            parts.append(dot(
+                jnp.concatenate([qh, qh, qt[1, :, k]], axis=1), jnp.concatenate([lo, hi, hi], axis=0)
+            ))
         g = parts[0] + swap_halves(parts[1])
         second[1 + c].put(0, beside(g[:128], swap_halves(g[128:])))
         second[1 + c].scatter()
@@ -440,7 +453,7 @@
     keep(zn, qc, jnp.concatenate([top[:, H:].T, low], axis=1))
     for c in s_sent + [q_sent] + d_sent:
         c.wait_send()
-    for c in first + second:
+    for c in first + lines:
         c.drain()
 
 
@@ -449,7 +462,8 @@
     s_cols = pl.ds(pl.multiple_of(odd * H, H), H)
     q_cols = pl.ds(pl.multiple_of((1 - odd) * H, H), H)
     stores = []
-    for i, rows in enumerate(tiles(R)):
+    for i in range(2):
+        rows = pl.ds(W * i, W)
         t = product(nh, rows, zh)
         out[0, rows, :] = t[:, :H]
         out[1, rows, :] = t[:, H:]
@@ -470,11 +484,11 @@
     for nb, more in CHUNKS1:
         t = (8 * nb + more, 128)
         bufs += [full(2, 8, *t), full(8, *t), full(8, *t), full(8, *t), full(2, 8, *t)]
-    for nb in CHUNKS2:
+    for nb in (LINE1, *CHUNKS2):
         t = (nb, 16, 128)
         bufs += [full(8, *t), full(8, *t), full(*t), full(*t), full(8, *t)]
     dma = lambda *n: pltpu.SemaphoreType.DMA(n)
-    n1, n2 = len(CHUNKS1), len(CHUNKS2)
+    n1, n2 = len(CHUNKS1), 1 + len(CHUNKS2)
     vmem = pl.BlockSpec(memory_space=pltpu.VMEM)
     new, root = pl.pallas_call(
         kernel,

time: 71 us -> 66.6 us (0.938); the launches traced: 70.9 us -> 65.6 us
  Pallas kernels: 70.1 us -> 64.8 us
    pallas_call x1, Pallas kernels: 67.4 us -> 61.9 us  [local(): pl.pallas_call(kernel, out_shape=[jax.ShapeDtypeStruct((2, R, W), BF16),...]
where the time goes in v4:
time: 66.6 us; the launch traced here: 65.6 us
  Pallas kernels  64.8 us (97%)
  between operations  0.82 us (1%)
    pallas_call x1, Pallas kernels, local(): pl.pallas_call(kernel, out_shape=[jax.ShapeDtypeStruct((2, R, W), BF16),...  61.9 us
    pallas_call x1, Pallas kernels, local(): pl.pallas_call(last, out_shape=jax.ShapeDtypeStruct((R, W), F32), in_spec...  2.82 us

profile of v4, /device:TPU:8, one launch (start us, length us, event | category | flops | bytes accessed | tf_op | source)
XLA Modules:
  0.0 65.6 jit_solution(13447922553429217617)
XLA Ops:
  0.7 61.9 %shard_map.28 = (bf16[2,1024,512]{2,1,0:T(8,128)(2,1)S(1)}, bf16[2,512,512]{2,1,0:T(8,128)(2,1)S(1)}) custom-call(f32[1024,512]{1,0:T(8,128)} %x_hbm.1, s32[1,1]{1,0:T(1,128)S(6)} %copy.3.mv_ref), custom_call_target="tpu_custom_call" | custom-call | tf_op jit(solution)/shard_map/pallas_call | solution.py:493
  62.6 2.8 %shard_map.29 = f32[1024,512]{1,0:T(8,128)} custom-call(bf16[2,1024,512]{2,1,0:T(8,128)(2,1)S(1)} %get-tuple-element.7.nh, bf16[2,512,512]{2,1,0:T(8,128)(2,1)S(1)} %get-tuple-element.8.zh), custom_call_target="tpu_custom_call" | custom-call | tf_op jit(solution)/shard_map/pallas_call | solution.py:515

commit v5 on v4

--- a/solution.py
+++ b/solution.py
@@ -17,7 +17,7 @@
 ROWS = 16384
 EPS = 1e-06
 T = 256
-CHUNKS1 = ((2, 0), (2, 0), (2, 2))
+CHUNKS1 = ((2, 0), (2, 0), (1, 2), (1, 2))
 LINE1 = 2
 CHUNKS2 = (2, 1, 1)
 
@@ -60,8 +60,6 @@
 
 
 def newton_schulz(a, ah, inv, a2, u, v, z2, z2h, yh):
-    for rows in tiles(W):
-        keep(ah, rows, a[rows, :])
     inv2 = inv * inv
     for rows, sq in zip(tiles(W), symmetric(ah, ah)):
         at = a[rows, :] * inv
@@ -287,17 +285,17 @@
     first[0].scatter_y()
     early.scatter()
     above, on = upper()
-    packed, diagonal = [], []
     for c, cols in enumerate((sc, qc)):
         m = mixed(cols, cols)
         g = square(cols, cols) + (m + m.T)
         first[1].put(c, g[:128, 128:])
         low = g[128:, 128:]
-        first[2].put(c, jnp.where(above | on, g[:128, :128], low))
-        diagonal.append(jnp.sum(jnp.where(on, low, 0.0), axis=0, keepdims=True))
-    first[2].put_rows(jnp.concatenate(diagonal, axis=0))
-    first[1].scatter_y()
-    first[2].scatter_y()
+        last_of = first[2 + c]
+        last_of.put(0, jnp.where(above | on, g[:128, :128], low))
+        diagonal = jnp.sum(jnp.where(on, low, 0.0), axis=0, keepdims=True)
+        last_of.put_rows(jnp.concatenate([diagonal, diagonal], axis=0))
+    for c in first[1:]:
+        c.scatter_y()
     for c in first:
         c.scatter_z()
     early.swap()
@@ -307,31 +305,33 @@
     for c in first:
         c.gather_y()
 
+    def place(i0, j0, b):
+        a[i0 : i0 + b.shape[0], j0 : j0 + b.shape[1]] = b
+        keep(ah, slice(i0, i0 + b.shape[0]), b, slice(j0, j0 + b.shape[1]))
+
+    def place_both(i0, j0, b):
+        place(i0, j0, b)
+        place(j0, i0, b.T)
+        return norm(b, 2.0)
+
     sq = jnp.zeros((8, 128), F32)
     for j in range(4):
         part = early if j < 2 else first[0]
         if j % 2 == 0:
             part.arrive()
-        i0, j0 = 128 * (j // 2), 128 * (j % 2)
-        b = part.get(j % 2)
-        sq = sq + norm(b, 2.0)
-        a[i0 : i0 + 128, H + j0 : H + j0 + 128] = b
-        a[H + j0 : H + j0 + 128, i0 : i0 + 128] = b.T
+        sq = sq + place_both(128 * (j // 2), H + 128 * (j % 2), part.get(j % 2))
     first[1].arrive()
     for c, o in ((0, 0), (1, H)):
-        b = first[1].get(c)
-        sq = sq + norm(b, 2.0)
-        a[o : o + 128, o + 128 : o + 256] = b
-        a[o + 128 : o + 256, o : o + 128] = b.T
-    first[2].arrive()
+        sq = sq + place_both(o, o + 128, first[1].get(c))
     for c, o in ((0, 0), (1, H)):
-        b = first[2].get(c)
+        first[2 + c].arrive()
+        b = first[2 + c].get(0)
         t = b.T
         b0 = jnp.where(above | on, b, t)
-        b2 = jnp.where(above, t, jnp.where(on, first[2].get_row(c), b))
+        b2 = jnp.where(above, t, jnp.where(on, first[2 + c].get_row(0), b))
         sq = sq + norm(b0, 1.0) + norm(b2, 1.0)
-        a[o : o + 128, o : o + 128] = b0
-        a[o + 128 : o + 256, o + 128 : o + 256] = b2
+        place(o, o, b0)
+        place(o + 128, o + 128, b2)
     scale = jnp.sqrt(jnp.sum(sq, keepdims=True) + EPS)
     inv = 1.0 / scale
     newton_schulz(a, ah, inv, a2, u, v, z2, z2h, yh)
@@ -426,23 +426,17 @@
         c.wait_recv()
     sq = jnp.zeros((8, 128), F32)
     for i, o in ((0, 0), (1, H)):
-        for rows in range(0, H, 128):
-            b = d_in[i, rows : rows + 128, :]
-            sq = sq + norm(b[:, :128], 1.0) + norm(b[:, 128:], 1.0)
-            a[o + rows : o + rows + 128, o : o + H] = b
-    def place(j, c, b):
-        i0, j0 = H + 128 * j, 128 * c
-        a[i0 : i0 + 128, j0 : j0 + 128] = b
-        a[j0 : j0 + 128, i0 : i0 + 128] = b.T
-        return norm(b, 2.0)
-
+        b = d_in[i]
+        sq = sq + norm(b[:, :128], 1.0) + norm(b[:, 128:], 1.0)
+        place(o, o, b)
     second[0].arrive()
     for j in range(2):
-        sq = sq + place(j, 0, second[0].get(j))
+        sq = sq + place_both(H + 128 * j, 0, second[0].get(j))
     for c in second[1:]:
         c.arrive()
     b0, b1 = second[1].get(0), second[2].get(0)
-    sq = sq + place(0, 1, beside(b0, swap_halves(b1))) + place(1, 1, beside(swap_halves(b0), b1))
+    sq = sq + place_both(H, 128, beside(b0, swap_halves(b1)))
+    sq = sq + place_both(H + 128, 128, beside(swap_halves(b0), b1))
     scale = jnp.sqrt(jnp.sum(sq, keepdims=True) + EPS)
     inv = 1.0 / scale
     newton_schulz(a, ah, inv, a2, u, v, z2, z2h, yh)

time: 66.6 us -> 66.8 us (level)
  the two profiles are of different devices: /device:TPU:8 before, /device:TPU:6 now
where the time goes in v5:
time: 66.8 us; the launch traced here: 66.7 us
  Pallas kernels  65.9 us (99%)
  between operations  0.82 us (1%)
    pallas_call x1, Pallas kernels, local(): pl.pallas_call(kernel, out_shape=[jax.ShapeDtypeStruct((2, R, W), BF16),...  63.1 us
    pallas_call x1, Pallas kernels, local(): pl.pallas_call(last, out_shape=jax.ShapeDtypeStruct((R, W), F32), in_spec...  2.83 us

profile of v5, /device:TPU:6, one launch (start us, length us, event | category | flops | bytes accessed | tf_op | source)
XLA Modules:
  0.0 66.7 jit_solution(235499896625122988)
XLA Ops:
  0.7 63.1 %shard_map.28 = (bf16[2,1024,512]{2,1,0:T(8,128)(2,1)S(1)}, bf16[2,512,512]{2,1,0:T(8,128)(2,1)S(1)}) custom-call(f32[1024,512]{1,0:T(8,128)} %x_hbm.1, s32[1,1]{1,0:T(1,128)S(6)} %copy.3.mv_ref), custom_call_target="tpu_custom_call" | custom-call | tf_op jit(solution)/shard_map/pallas_call | solution.py:487
  63.7 2.8 %shard_map.29 = f32[1024,512]{1,0:T(8,128)} custom-call(bf16[2,1024,512]{2,1,0:T(8,128)(2,1)S(1)} %get-tuple-element.7.nh, bf16[2,512,512]{2,1,0:T(8,128)(2,1)S(1)} %get-tuple-element.8.zh), custom_call_target="tpu_custom_call" | custom-call | tf_op jit(solution)/shard_map/pallas_call | solution.py:509

commit v6 on v4

--- a/solution.py
+++ b/solution.py
@@ -247,17 +247,17 @@
     ]
     early, second = lines[0], lines[1:]
 
+    barrier = pltpu.get_barrier_semaphore()
+    z, y = r // 2, lax.rem(r, 2)
+    for row in [lax.rem(z + d, 8) * 2 + y for d in ORDER_Z] + [r + 1 - 2 * y]:
+        pl.semaphore_signal(barrier, inc=1, device_id={"row": row}, device_id_type=MESH)
+    for to in (slow, quick):
+        pl.semaphore_signal(barrier, inc=1, device_id={"pair": to}, device_id_type=MESH)
     loads = []
     for i, rows in enumerate(tiles(R)):
         c = pltpu.make_async_copy(x_hbm.at[rows], x.at[rows], load_sem.at[i])
         c.start()
         loads.append(c)
-    barrier = pltpu.get_barrier_semaphore()
-    z, y = r // 2, lax.rem(r, 2)
-    for row in [lax.rem(z + d, 8) * 2 + y for d in range(1, 8)] + [r + 1 - 2 * y]:
-        pl.semaphore_signal(barrier, inc=1, device_id={"row": row}, device_id_type=MESH)
-    for to in (slow, quick):
-        pl.semaphore_signal(barrier, inc=1, device_id={"pair": to}, device_id_type=MESH)
 
     lead_slow = (mv_ref[...] + odd) == 1
     for i, rows in enumerate(tiles(R)):
@@ -412,14 +412,14 @@
         g = parts[0] + swap_halves(parts[1])
         second[1 + c].put(0, beside(g[:128], swap_halves(g[128:])))
         second[1 + c].scatter()
+    second[0].swap()
+    second[1].swap()
+    second[0].gather()
+    second[1].gather()
     for i, rows in enumerate(tiles(W)):
         p0, p1 = p_in[0, rows, :], p_in[1, rows, :]
         keep(nh, rows, beside(p0, swap_halves(p1)), pl.ds(128, 128))
         keep(nh, pl.ds(W + i * T, T), beside(swap_halves(p0), p1), pl.ds(128, 128))
-    second[0].swap()
-    second[1].swap()
-    second[0].gather()
-    second[1].gather()
     second[2].swap()
     second[2].gather()
     for c in d_sent:

time: 66.6 us -> 66.4 us (level)
  no operation moved by 1% of the time
where the time goes in v6:
time: 66.4 us; the launch traced here: 65.4 us
  Pallas kernels  64.6 us (97%)
  between operations  0.82 us (1%)
    pallas_call x1, Pallas kernels, local(): pl.pallas_call(kernel, out_shape=[jax.ShapeDtypeStruct((2, R, W), BF16),...  61.7 us
    pallas_call x1, Pallas kernels, local(): pl.pallas_call(last, out_shape=jax.ShapeDtypeStruct((R, W), F32), in_spec...  2.83 us

profile of v6, /device:TPU:8, one launch (start us, length us, event | category | flops | bytes accessed | tf_op | source)
XLA Modules:
  0.0 65.4 jit_solution(8253514463003112012)
XLA Ops:
  0.7 61.7 %shard_map.28 = (bf16[2,1024,512]{2,1,0:T(8,128)(2,1)S(1)}, bf16[2,512,512]{2,1,0:T(8,128)(2,1)S(1)}) custom-call(f32[1024,512]{1,0:T(8,128)} %x_hbm.1, s32[1,1]{1,0:T(1,128)S(6)} %copy.3.mv_ref), custom_call_target="tpu_custom_call" | custom-call | tf_op jit(solution)/shard_map/pallas_call | solution.py:493
  62.4 2.8 %shard_map.29 = f32[1024,512]{1,0:T(8,128)} custom-call(bf16[2,1024,512]{2,1,0:T(8,128)(2,1)S(1)} %get-tuple-element.7.nh, bf16[2,512,512]{2,1,0:T(8,128)(2,1)S(1)} %get-tuple-element.8.zh), custom_call_target="tpu_custom_call" | custom-call | tf_op jit(solution)/shard_map/pallas_call | solution.py:515
